TPU v7x, 32 devices: a whole 2x2x4 slice. The times are simulated.
32 devices in a mesh: groups: 2 (over y), train: 8 (over z, x), query: 2 (over core).
Axes of the slice: x: 2, y: 2, z: 4, core: 2. Of those that a mesh axis runs over, the one named last changes fastest.
Arguments:
- train_grads: bfloat16 [12288, 4096], P(('groups', 'train'), 'query'), parts along dimension 0, may hold values from -6 to 6
- query_grads: bfloat16 [512, 4096], P(('groups', 'train'), 'query'), parts along dimension 0, may hold values from -6 to 6
- precond: bfloat16 [8, 512, 512], P('query'), may hold values from -0.25 to 0.25
- pairs: int32 [96, 2], P(('groups', 'train')), parts along dimension 0, may hold values from 0 to 7, all different within a row; in each aligned block of 6 rows (0 to 5, 6 to 11, ...) at most 3 rows name the same one
Outputs:
- top_scores: float32 [512, 16], P(('groups', 'train', 'query')), parts along dimension 0
There are 2 independent parts, one for each index of `groups`. A program takes and returns all parts, laid end to end along the dimension named above; an argument that names none is the same for every part. Nothing has to cross between parts.
Inputs may be any that keep to these rules, and one draw needn't show every extreme that they name: `pairs`: each row names 2 different query blocks. Within each aligned block of 6 rows (the training blocks of one index of train) no query block is named more than 3 times, and some query block exactly 3 times. Every query block is named by some row.
All inputs are finite; a program needn't handle non-finite values.
Results may differ from a plain program's by a relative error of at most 0.0014.
Values may be sent and summed in bfloat16 or wider, within the bound.
A program may use at most 64 MiB of HBM per device.

v0:
```python
import math

import jax
import jax.numpy as jnp
from jax import lax
from jax.sharding import PartitionSpec as P

K = 4096
TBLK = 128
TOPM = 16
MOST = 3


empty_fill = -1e30


def per_device(train_grads, query_grads, precond, pairs):
    width_blocks = precond.shape[0]
    block_size = precond.shape[1]
    local_queries = query_grads.shape[0]
    owners = lax.axis_size("train")
    rows_local = train_grads.shape[0]
    train_blocks = rows_local // TBLK
    factor = 1.0 / math.sqrt(K)
    shaped = query_grads.reshape(local_queries, width_blocks, block_size)
    conditioned = jnp.einsum("qbk,bkj->qbj", shaped, precond, preferred_element_type=jnp.float32)
    conditioned = conditioned.astype(jnp.bfloat16).reshape(local_queries, width_blocks * block_size)
    partial_scores = lax.dot_general(
        lax.all_gather(conditioned, "train", axis=0, tiled=True),
        train_grads,
        (((1,), (1,)), ((), ())),
        preferred_element_type=jnp.float32,
    )
    targets = lax.broadcasted_iota(jnp.int32, (1, 1, owners), 2)
    counted = jnp.sum((pairs[:, :, None] == targets).astype(jnp.int32), axis=1)
    earlier = jnp.cumsum(counted, axis=0) - counted
    slot_ids = lax.broadcasted_iota(jnp.int32, (1, 1, MOST), 2)
    select = (counted[:, :, None] * (earlier[:, :, None] == slot_ids).astype(jnp.int32)).astype(
        jnp.float32
    )
    filled = jnp.sum(select, axis=0)
    shaped_scores = partial_scores.reshape(owners, local_queries, train_blocks, TBLK)
    score_tiles = jnp.einsum(
        "bds,dqbr->dsqr", select, shaped_scores, precision=lax.Precision.HIGHEST
    )
    score_tiles = score_tiles * factor + ((1.0 - filled) * empty_fill)[:, :, None, None]
    partial_tiles = lax.all_to_all(score_tiles, "train", split_axis=0, concat_axis=0, tiled=True)
    arrived = lax.psum_scatter(partial_tiles, "query", scatter_dimension=2, tiled=True)
    kept_rows = arrived.shape[2]
    candidates = jnp.transpose(arrived, (2, 0, 1, 3)).reshape(kept_rows, -1)
    return lax.top_k(candidates, TOPM)[0]


def solution(mesh):
    placed = (
        P(("groups", "train"), "query"),
        P(("groups", "train"), "query"),
        P("query", None, None),
        P(("groups", "train"), None),
    )
    return jax.shard_map(
        per_device,
        mesh=mesh,
        in_specs=placed,
        out_specs=P(("groups", "train", "query"), None),
        check_vma=False,
    )
```

profile of v0, /device:TPU:0, one launch (start us, length us, event | category | flops | bytes accessed | tf_op | source)
XLA Modules:
  0.0 102.7 jit_solution(8633644895168647402)
XLA Ops:
  6.5 0.0 copy-start
  6.5 0.0 all-gather.2.cloned.1.call-start
  6.5 2.2 %fusion.1 = bf16[4,4,8,512]{3,2,1,0:T(8,128)(2,1)S(1)} fusion(bf16[4,512,512]{2,1,0:T(8,128)(2,1)} %param.6, bf16[4,4,8,512]{3,2,1,0:T(8,128)(2,1)} %bitcast.20), kind=kOutput, calls=%fused_computation.3 | convolution fusion | flops 67174400 | bytes 2359296 | tf_op jit(solution)/shard_map/qbk,bkj->qbj/dot_general | solution.py:26
  8.8 0.7 copy.27
  9.5 0.0 all-gather.2.cloned.1.call-update
  9.5 0.0 reduce-scatter.2.cloned.1.call-start
  9.5 0.8 copy.17
  10.3 0.1 fusion.10
  10.4 0.1 copy.19
  10.5 0.1 copy.18
  10.6 0.1 convert_reduce_fusion
  10.7 41.8 %all-gather.2.cloned.1.call-done = bf16[256,2048]{1,0:T(8,128)(2,1)} async-done(((bf16[32,2048]{1,0:T(8,128)(2,1)}), bf16[256,2048]{1,0:T(8,128)(2,1)}) %all-gather.2.cloned.1.call-update) | async-done | bytes 1048592 | tf_op jit(solution)/shard_map/all_gather | solution.py:29
  52.5 0.0 copy-done
  52.5 3.2 %fusion.12 = f32[256,768]{1,0:T(8,128)} fusion(bf16[256,2048]{1,0:T(8,128)(2,1)} %all-gather.2.cloned.1.call-done, bf16[768,2048]{1,0:T(8,128)(2,1)S(1)} %copy-done), kind=kOutput, calls=%fused_computation.18 | convolution fusion | flops 805306368 | bytes 4980736 | tf_op jit(solution)/shard_map/dot_general | solution.py:28
  55.7 2.2 %reshape.29 = f32[8,32,6,128]{3,2,1,0:T(8,128)} reshape(f32[256,768]{1,0:T(8,128)} %fusion.12) | data formatting | bytes 1572864 | tf_op jit(solution)/shard_map/reshape | solution.py:42
  57.9 2.2 %fusion = f32[8,3,32,128]{3,1,2,0:T(4,128)S(1)} fusion(f32[8,32,6,128]{3,2,1,0:T(8,128)} %reshape.29, f32[8,3]{1,0:T(8,128)S(1)} %subtract_multiply_fusion, s32[6,8]{0,1:T(8,128)S(1)} %copy.19, s32[6,8]{0,1:T(8,128)S(1)} %copy.18), kind=kOutput, calls=%fused_computation.1 | convolution fusion | flops 7274928 | bytes 1180128 | tf_op jit(solution)/shard_map/bds,dqbr->dsqr/dot_general | solution.py:43
  60.2 13.7 %all_to_all.5 = f32[8,3,32,128]{3,2,1,0:T(8,128)S(1)} all-to-all(f32[8,3,32,128]{3,2,1,0:T(8,128)S(1)} %copy.22), channel_id=1, replica_groups=mesh['groups'=2,'train'=8,'query'=2] {'train'}, dimensions={0} | all-to-all | bytes 786432 | tf_op jit(solution)/shard_map/all_to_all | solution.py:47
  73.9 1.0 copy.23
  74.8 0.0 reduce-scatter.2.cloned.1.call-update
  74.9 6.6 %reduce-scatter.2.cloned.1.call-done = f32[8,3,16,128]{3,0,1,2:T(8,128)} async-done(((f32[8,3,32,128]{3,0,1,2:T(8,128)}), f32[8,3,16,128]{3,0,1,2:T(8,128)}) %reduce-scatter.2.cloned.1.call-update) | async-done | bytes 196624 | tf_op jit(solution)/shard_map/reduce_scatter | solution.py:48
  81.5 1.0 copy.24
  82.5 0.8 reshape.30
  83.3 12.6 %top_k.7 = (f32[16,16]{1,0:T(8,128)}, s32[16,16]{1,0:T(8,128)}) custom-call(f32[16,3072]{1,0:T(8,128)} %reshape.30), custom_call_target="TopK", called_computations={%compare_greater_than.1.5.clone.clone} | custom-call | tf_op jit(solution)/shard_map/top_k | solution.py:51
  (4 shorter events, 0.1 us)
Async XLA Ops:
  6.5 46.0 %copy-start = (bf16[768,2048]{1,0:T(8,128)(2,1)S(1)}, bf16[768,2048]{1,0:T(8,128)(2,1)}, u32[]{:S(2)}) copy-start(bf16[768,2048]{1,0:T(8,128)(2,1)} %param.4) | copy-start | bytes 9437188
  6.5 45.9 %all-gather.2.cloned.1.call-start = ((), (), s32[]{:S(2)}) async-start(), calls=%async_computation.2 | async-start | bytes 1179648 | tf_op jit(solution)/shard_map/all_gather | solution.py:29
  9.5 72.0 %reduce-scatter.2.cloned.1.call-start = ((), (), s32[]{:S(2)}) async-start(), calls=%async_computation.3 | async-start | bytes 589824 | tf_op jit(solution)/shard_map/reduce_scatter | solution.py:48
Sparse Core Ops, SparseCore 0:
  9.6 42.8 all-gather.1
  75.0 6.4 reduce-scatter.1
where the time goes:
time: 103 us
  waiting for transfers between devices  48.5 us (47%)
  blocking collectives  13.7 us (13%)
  between operations  13.4 us (13%)
  other arithmetic  12.8 us (12%)
  matrix products  7.6 us (7%)
  local copies, waits for them, and re-layouts  6.63 us (6%)
    all_gather x1, waiting for transfers between devices, per_device(): lax.all_gather(conditioned, 'train', axis=0, tiled=True)  41.8 us
    all_to_all x1, blocking collectives, per_device(): lax.all_to_all(score_tiles, 'train', split_axis=0, concat_axis=0, tiled=T...  13.7 us
    top_k x1, other arithmetic, per_device(): return lax.top_k(candidates, TOPM)[0]  12.6 us
    reduce_scatter x1, waiting for transfers between devices, per_device(): lax.psum_scatter(partial_tiles, 'query', scatter_dimension=2, tiled=True)  6.64 us
    dot_general x1, matrix products, per_device(): lax.dot_general(lax.all_gather(conditioned, 'train', axis=0, tiled=True),...  3.17 us
    reshape x1, local copies, waits for them, and re-layouts, per_device(): partial_scores.reshape(owners, local_queries, train_blocks, TBLK)  2.24 us
    dot_general x1, matrix products, per_device(): jnp.einsum('qbk,bkj->qbj', shaped, precond, preferred_element_type=jnp.fl...  2.23 us
    dot_general x1, matrix products, per_device(): jnp.einsum('bds,dqbr->dsqr', select, shaped_scores, precision=lax.Precisi...  2.21 us
  transfers between devices with their start and end apart: 2, of which 2 were waited for; matrix products, arithmetic and copies ran while one was open for 1% of the time, Pallas kernels for 0%

commit v1 on v0

v1 whole, which is shorter than its diff:
```python
import functools
import math

import jax
import jax.numpy as jnp
from jax import lax
from jax.experimental import pallas as pl
from jax.experimental.pallas import tpu as pltpu
from jax.sharding import PartitionSpec as P

K = 4096
TBLK = 128
TOPM = 16
LANES = 128
MESH = pl.DeviceIdType.MESH

empty_fill = -1e30


def exchange(xs, i, j):
    a, b = xs[i], xs[j]
    xs[i], xs[j] = jnp.maximum(a, b), jnp.minimum(a, b)


def sort_falling(xs):
    xs = list(xs)
    n = len(xs)
    p = 1
    while p < n:
        k = p
        while k >= 1:
            for j in range(k % p, n - k, 2 * k):
                for i in range(min(k, n - j - k)):
                    if (i + j) // (2 * p) == (i + j + k) // (2 * p):
                        exchange(xs, i + j, i + j + k)
            k //= 2
        p *= 2
    return xs


def merge_top(xs, ys):
    n = len(xs)
    out = [jnp.maximum(xs[i], ys[n - 1 - i]) for i in range(n)]
    step = n // 2
    while step >= 1:
        for i in range(n):
            if i & step == 0:
                exchange(out, i, i + step)
        step //= 2
    return out


def merge_sublanes(xs):
    for shift in (4, 2, 1):
        xs = merge_top(xs, [pltpu.roll(x, shift, 0) for x in xs])
    return xs


def kernel(
    owners, columns, chunks,
    query_hbm, precond_hbm, train_hbm, pairs_ref, out_ref,
    query_v, precond_v, train_v, gathered, outgoing, incoming, scores, tops, arrived, flipped,
    load_sem, send_sem, recv_sem, pair_send, pair_recv, top_send, top_recv,
):
    me = lax.axis_index("train")
    core = lax.axis_index("query")
    x, z = lax.rem(me, columns), me // columns
    levels = owners // columns
    width = query_v.shape[1]
    chunk = width // chunks
    size = precond_v.shape[1]
    half = query_v.shape[0] // 2
    train_blocks = train_v.shape[0] // TBLK
    groups = owners * half // LANES
    per_group = LANES // half

    loads = [
        pltpu.make_async_copy(query_hbm, query_v, load_sem.at[0]),
        pltpu.make_async_copy(precond_hbm, precond_v, load_sem.at[1]),
        pltpu.make_async_copy(train_hbm, train_v, load_sem.at[2]),
    ]
    for load in loads:
        load.start()

    barrier = pltpu.get_barrier_semaphore()

    def greet(step, carry):
        pl.semaphore_signal(
            barrier, inc=1, device_id={"train": lax.rem(me + step, owners)}, device_id_type=MESH
        )
        return carry

    lax.fori_loop(1, owners, greet, 0)
    pl.semaphore_signal(barrier, inc=1, device_id={"query": 1 - core}, device_id_type=MESH)

    loads[0].wait()
    loads[1].wait()
    for j in range(precond_v.shape[0]):
        part = jnp.dot(
            query_v[:, j * size:(j + 1) * size], precond_v[j], preferred_element_type=jnp.float32
        ).astype(jnp.bfloat16)
        gathered[0, me, :, j * size:(j + 1) * size] = part[:half]
        gathered[1, me, :, j * size:(j + 1) * size] = part[half:]
    pl.semaphore_wait(barrier, owners)

    def piece(owner, k, way, peer):
        ref = gathered.at[:, owner, :, pl.ds(k * chunk, chunk)]
        return pltpu.make_async_remote_copy(
            src_ref=ref, dst_ref=ref,
            send_sem=send_sem.at[way, owner, k], recv_sem=recv_sem.at[owner, k],
            device_id={"train": peer}, device_id_type=MESH,
        )

    def across(owner, k, act):
        for j in range(1, columns):
            act(piece(owner, k, 1 + j, z * columns + lax.rem(x + j, columns)))

    def upward(owner, k, act):
        @pl.when(z < levels - 1)
        def _():
            act(piece(owner, k, 0, me + columns))

    def downward(owner, k, act):
        @pl.when(z > 0)
        def _():
            act(piece(owner, k, 1, me - columns))

    start = lambda copy: copy.start()
    sent = lambda copy: copy.wait_send()
    landed = lambda copy: copy.wait_recv()

    for k in range(chunks):
        upward(me, k, start)
        downward(me, k, start)
        across(me, k, start)

    def relay(hop, carry):
        for k in range(chunks):
            @pl.when(z - hop >= 0)
            def _():
                owner = me - hop * columns
                landed(piece(owner, k, 0, me))
                upward(owner, k, start)
                across(owner, k, start)

            @pl.when(z + hop < levels)
            def _():
                owner = me + hop * columns
                landed(piece(owner, k, 1, me))
                downward(owner, k, start)
                across(owner, k, start)
        return carry

    lax.fori_loop(1, levels, relay, 0)

    def collect(level, carry):
        for j in range(1, columns):
            for k in range(chunks):
                landed(piece(level * columns + lax.rem(x + j, columns), k, 1 + j, me))
        return carry

    lax.fori_loop(0, levels, collect, 0)
    loads[2].wait()

    def trade(g):
        return pltpu.make_async_remote_copy(
            src_ref=outgoing.at[g], dst_ref=incoming.at[g],
            send_sem=pair_send.at[g], recv_sem=pair_recv.at[g],
            device_id={"query": 1 - core}, device_id_type=MESH,
        )

    def product(which, g):
        rows = gathered[which, pl.ds(g * per_group, per_group)].reshape(LANES, width)
        return lax.dot_general(
            train_v[...], rows, (((1,), (1,)), ((), ())), preferred_element_type=jnp.float32
        )

    def first(g, carry):
        outgoing[g] = product(1 - core, g)
        trade(g).start()
        return carry

    lax.fori_loop(0, groups, first, 0)

    def best_of(g, carry):
        scores[...] = product(core, g)
        trade(g).wait()
        lane_owner = g * per_group + lax.broadcasted_iota(jnp.int32, (8, LANES), 1) // half

        def visit(b, best):
            named = lane_owner == pairs_ref[b, 0]
            for f in range(1, pairs_ref.shape[1]):
                named = named | (lane_owner == pairs_ref[b, f])
            vals = []
            for i in range(TBLK // 8):
                at = pl.ds(pl.multiple_of(b * TBLK + i * 8, 8), 8)
                total = scores[at, :] + incoming[g, at, :]
                vals.append(jnp.where(named, total, empty_fill))
            return tuple(merge_top(list(best), sort_falling(vals)))

        none = tuple(jnp.full((8, LANES), empty_fill, jnp.float32) for _ in range(TOPM))
        best = merge_sublanes(list(lax.fori_loop(0, train_blocks, visit, none)))
        tops[g] = jnp.concatenate([v[:1] for v in best], axis=0)
        return carry

    lax.fori_loop(0, groups, best_of, 0)

    def deliver(step):
        peer = lax.rem(me + step, owners)
        return pltpu.make_async_remote_copy(
            src_ref=tops.at[peer // per_group], dst_ref=arrived.at[me],
            send_sem=top_send.at[peer], recv_sem=top_recv.at[me],
            device_id={"train": peer}, device_id_type=MESH,
        )

    def receive(step):
        peer = lax.rem(me + step, owners)
        return pltpu.make_async_remote_copy(
            src_ref=tops.at[0], dst_ref=arrived.at[peer],
            send_sem=top_send.at[peer], recv_sem=top_recv.at[peer],
            device_id={"train": peer}, device_id_type=MESH,
        )

    def each(act):
        def body(step, carry):
            act(step)
            return carry
        lax.fori_loop(1, owners, body, 0)

    each(lambda step: deliver(step).start())
    arrived[me] = tops[me // per_group]
    for k in range(chunks):
        upward(me, k, sent)
        downward(me, k, sent)
        across(me, k, sent)

    def drain(hop, carry):
        for k in range(chunks):
            @pl.when(z - hop >= 0)
            def _():
                upward(me - hop * columns, k, sent)
                across(me - hop * columns, k, sent)

            @pl.when(z + hop < levels)
            def _():
                downward(me + hop * columns, k, sent)
                across(me + hop * columns, k, sent)
        return carry

    lax.fori_loop(1, levels, drain, 0)
    each(lambda step: receive(step).wait_recv())

    best = None
    for s in range(owners // 8):
        lists = [arrived[s * 8:(s + 1) * 8, r, :] for r in range(TOPM)]
        best = lists if best is None else merge_top(best, lists)
    best = merge_sublanes(best)
    ranked = jnp.concatenate([v[:1] for v in best], axis=0) * (1.0 / math.sqrt(K))
    square = jnp.concatenate(
        [ranked, jnp.zeros((LANES - TOPM, LANES), jnp.float32)], axis=0
    )
    flipped[...] = square.T
    mine = pl.multiple_of(lax.rem(me, per_group) * half, half)
    out_ref[...] = flipped[pl.ds(mine, half), :TOPM]
    each(lambda step: deliver(step).wait_send())


def per_device(train_grads, query_grads, precond, pairs):
    owners = lax.axis_size("train")
    columns = 1
    for c in range(2, owners):
        if owners % c == 0 and c ** 3 <= owners:
            columns = c
    queries, width = query_grads.shape
    rows = train_grads.shape[0]
    chunks = 4 if owners <= 8 else 1
    half = queries // 2
    groups = owners * half // LANES
    f32 = jnp.float32
    return pl.pallas_call(
        functools.partial(kernel, owners, columns, chunks),
        out_shape=jax.ShapeDtypeStruct((half, TOPM), f32),
        in_specs=[pl.BlockSpec(memory_space=pl.ANY)] * 3
        + [pl.BlockSpec(memory_space=pltpu.SMEM)],
        out_specs=pl.BlockSpec(memory_space=pltpu.VMEM),
        scratch_shapes=[
            pltpu.VMEM(query_grads.shape, query_grads.dtype),
            pltpu.VMEM(precond.shape, precond.dtype),
            pltpu.VMEM(train_grads.shape, train_grads.dtype),
            pltpu.VMEM((2, owners, half, width), jnp.bfloat16),
            pltpu.VMEM((groups, rows, LANES), f32),
            pltpu.VMEM((groups, rows, LANES), f32),
            pltpu.VMEM((rows, LANES), f32),
            pltpu.VMEM((groups, TOPM, LANES), f32),
            pltpu.VMEM((owners, TOPM, LANES), f32),
            pltpu.VMEM((LANES, LANES), f32),
            pltpu.SemaphoreType.DMA((3,)),
            pltpu.SemaphoreType.DMA((1 + columns, owners, chunks)),
            pltpu.SemaphoreType.DMA((owners, chunks)),
            pltpu.SemaphoreType.DMA((groups,)),
            pltpu.SemaphoreType.DMA((groups,)),
            pltpu.SemaphoreType.DMA((owners,)),
            pltpu.SemaphoreType.DMA((owners,)),
        ],
        compiler_params=pltpu.CompilerParams(
            collective_id=0, has_side_effects=True, vmem_limit_bytes=48 * 1024 * 1024
        ),
    )(query_grads, precond, train_grads, pairs)


def solution(mesh):
    placed = (
        P(("groups", "train"), "query"),
        P(("groups", "train"), "query"),
        P("query", None, None),
        P(("groups", "train"), None),
    )
    return jax.shard_map(
        per_device,
        mesh=mesh,
        in_specs=placed,
        out_specs=P(("groups", "train", "query"), None),
        check_vma=False,
    )
```

time: 103 us -> 35.4 us (0.34)
  waiting for transfers between devices: 48.5 us -> 0 us
  Pallas kernels: 0 us -> 29.4 us
  blocking collectives: 13.7 us -> 0 us
  between operations: 13.4 us -> 0.01 us
  other arithmetic: 12.8 us -> 0 us
  matrix products: 7.6 us -> 0 us
    all_gather x1 -> x0, waiting for transfers between devices: 41.8 us -> none  [per_device(): lax.all_gather(conditioned, 'train', axis=0, tiled=True)]
    pallas_call x0 -> x1, Pallas kernels: none -> 29.4 us  [per_device(): pl.pallas_call(functools.partial(kernel, owners, columns, chunks), out_sh...]
    all_to_all x1 -> x0, blocking collectives: 13.7 us -> none  [per_device(): lax.all_to_all(score_tiles, 'train', split_axis=0, concat_axis=0, tiled=T...]
    top_k x1 -> x0, other arithmetic: 12.6 us -> none  [per_device(): return lax.top_k(candidates, TOPM)[0]]
    dot_general x3 -> x0, matrix products: 7.6 us -> none  [the longest x1 3.17 us: per_device(): lax.dot_general(lax.all_gather(conditioned, 'train', axis=0, tiled=True),...]
    reduce_scatter x1 -> x0, waiting for transfers between devices: 6.64 us -> none  [per_device(): lax.psum_scatter(partial_tiles, 'query', scatter_dimension=2, tiled=True)]
    unnamed x3 -> x8, local copies, waits for them, and re-layouts: 0.77 us -> 5.75 us
    reshape x3 -> x0, local copies, waits for them, and re-layouts: 3.69 us -> none  [the longest x1 2.24 us: per_device(): partial_scores.reshape(owners, local_queries, train_blocks, TBLK)]
  transfers between devices with their start and end apart: 2 -> 0, of which waited for: 2 -> 0; matrix products, arithmetic and copies ran while one was open for 1% -> 0% of each run, Pallas kernels for 0% -> 0%
where the time goes in v1:
time: 35.4 us; the launch traced here: 35.2 us
  Pallas kernels  29.4 us (83%)
  local copies, waits for them, and re-layouts  5.75 us (16%)
    pallas_call x1, Pallas kernels, per_device(): pl.pallas_call(functools.partial(kernel, owners, columns, chunks), out_sh...  29.4 us
    unnamed x8, local copies, waits for them, and re-layouts  5.75 us

profile of v1, /device:TPU:0, one launch (start us, length us, event | category | flops | bytes accessed | tf_op | source)
XLA Modules:
  0.0 35.2 jit_solution(3908377147556853118)
XLA Ops:
  0.0 0.8 %copy.5.pairs_ref = s32[6,2]{1,0:T(8,128)S(1)} copy(s32[6,2]{0,1:T(2,128)} %param.7) | data formatting | bytes 96 | tf_op args[3]
  0.8 0.0 copy-start
  0.8 1.9 %copy-done = bf16[768,2048]{1,0:T(8,128)(2,1)S(1)} copy-done((bf16[768,2048]{1,0:T(8,128)(2,1)S(1)}, bf16[768,2048]{1,0:T(8,128)(2,1)}, u32[]{:S(2)}) %copy-start) | copy-done | bytes 3145752
  2.7 0.0 copy-start.1
  2.7 1.6 %copy-done.1 = bf16[4,512,512]{2,1,0:T(8,128)(2,1)S(1)} copy-done((bf16[4,512,512]{2,1,0:T(8,128)(2,1)S(1)}, bf16[4,512,512]{2,1,0:T(8,128)(2,1)}, u32[]{:S(2)}) %copy-start.1) | copy-done | bytes 2097176
  4.2 0.0 copy-start.2
  4.2 0.9 %copy-done.2 = bf16[32,2048]{1,0:T(8,128)(2,1)S(1)} copy-done((bf16[32,2048]{1,0:T(8,128)(2,1)S(1)}, bf16[32,2048]{1,0:T(8,128)(2,1)}, u32[]{:S(2)}) %copy-start.2) | copy-done | bytes 131096
  5.2 29.4 %shard_map.46 = f32[16,16]{1,0:T(8,128)S(1)} custom-call(bf16[32,2048]{1,0:T(8,128)(2,1)S(1)} %copy-done.2, bf16[4,512,512]{2,1,0:T(8,128)(2,1)S(1)} %copy-done.1, bf16[768,2048]{1,0:T(8,128)(2,1)S(1)} %copy-done, s32[6,2]{1,0:T(8,128)S(1)} %copy.5.pairs_ref), custom_call_target="tpu_custom_call" | custom-call | tf_op jit(solution)/shard_map/pallas_call | solution.py:280
  34.6 0.6 %copy.7 = f32[16,16]{1,0:T(8,128)} copy(f32[16,16]{1,0:T(8,128)S(1)} %shard_map.46) | data formatting | bytes 2048
Async XLA Ops:
  0.8 1.9 %copy-start = (bf16[768,2048]{1,0:T(8,128)(2,1)S(1)}, bf16[768,2048]{1,0:T(8,128)(2,1)}, u32[]{:S(2)}) copy-start(bf16[768,2048]{1,0:T(8,128)(2,1)} %train_hbm.1) | copy-start | bytes 9437188
  2.7 1.6 %copy-start.1 = (bf16[4,512,512]{2,1,0:T(8,128)(2,1)S(1)}, bf16[4,512,512]{2,1,0:T(8,128)(2,1)}, u32[]{:S(2)}) copy-start(bf16[4,512,512]{2,1,0:T(8,128)(2,1)} %precond_hbm.1) | copy-start | bytes 6291460
  4.2 0.9 %copy-start.2 = (bf16[32,2048]{1,0:T(8,128)(2,1)S(1)}, bf16[32,2048]{1,0:T(8,128)(2,1)}, u32[]{:S(2)}) copy-start(bf16[32,2048]{1,0:T(8,128)(2,1)} %query_hbm.1) | copy-start | bytes 393220

commit v2 on v1

--- a/solution.py
+++ b/solution.py
@@ -58,8 +58,8 @@
 
 def kernel(
     owners, columns, chunks,
-    query_hbm, precond_hbm, train_hbm, pairs_ref, out_ref,
-    query_v, precond_v, train_v, gathered, outgoing, incoming, scores, tops, arrived, flipped,
+    query_hbm, precond_hbm, train_hbm, pairs_hbm, out_ref,
+    pairs_ref, query_v, precond_v, train_v, gathered, outgoing, incoming, scores, tops, arrived,
     load_sem, send_sem, recv_sem, pair_send, pair_recv, top_send, top_recv,
 ):
     me = lax.axis_index("train")
@@ -78,19 +78,20 @@
         pltpu.make_async_copy(query_hbm, query_v, load_sem.at[0]),
         pltpu.make_async_copy(precond_hbm, precond_v, load_sem.at[1]),
         pltpu.make_async_copy(train_hbm, train_v, load_sem.at[2]),
+        pltpu.make_async_copy(pairs_hbm, pairs_ref, load_sem.at[3]),
     ]
     for load in loads:
         load.start()
 
     barrier = pltpu.get_barrier_semaphore()
 
-    def greet(step, carry):
-        pl.semaphore_signal(
-            barrier, inc=1, device_id={"train": lax.rem(me + step, owners)}, device_id_type=MESH
-        )
-        return carry
-
-    lax.fori_loop(1, owners, greet, 0)
+    def greet(peer):
+        pl.semaphore_signal(barrier, inc=1, device_id={"train": peer}, device_id_type=MESH)
+
+    pl.when(z > 0)(lambda: greet(me - columns))
+    pl.when(z < levels - 1)(lambda: greet(me + columns))
+    for j in range(1, columns):
+        greet(z * columns + lax.rem(x + j, columns))
     pl.semaphore_signal(barrier, inc=1, device_id={"query": 1 - core}, device_id_type=MESH)
 
     loads[0].wait()
@@ -101,7 +102,8 @@
         ).astype(jnp.bfloat16)
         gathered[0, me, :, j * size:(j + 1) * size] = part[:half]
         gathered[1, me, :, j * size:(j + 1) * size] = part[half:]
-    pl.semaphore_wait(barrier, owners)
+    below, above = (z + levels - 1) // levels, (2 * levels - 2 - z) // levels
+    pl.semaphore_wait(barrier, columns + below + above)
 
     def piece(owner, k, way, peer):
         ref = gathered.at[:, owner, :, pl.ds(k * chunk, chunk)]
@@ -161,6 +163,7 @@
 
     lax.fori_loop(0, levels, collect, 0)
     loads[2].wait()
+    loads[3].wait()
 
     def trade(g):
         return pltpu.make_async_remote_copy(
@@ -181,6 +184,19 @@
         return carry
 
     lax.fori_loop(0, groups, first, 0)
+
+    def slot(owner):
+        return owner // per_group * per_group + per_group - 1 - lax.rem(owner, per_group)
+
+    def tops_of(g, best):
+        place = lax.broadcasted_iota(jnp.int32, (8, LANES), 1) // half
+        for h in range(TOPM // per_group):
+            packed = None
+            for i in range(per_group):
+                turned = pltpu.roll(best[h * per_group + i], (i + 1) * half % LANES, 1)
+                turned = pltpu.roll(turned, 0, 1, stride=half, stride_axis=0)
+                packed = turned if packed is None else jnp.where(place == i, turned, packed)
+            tops[pl.ds(g * per_group, per_group), h, :] = packed
 
     def best_of(g, carry):
         scores[...] = product(core, g)
@@ -200,7 +216,7 @@
 
         none = tuple(jnp.full((8, LANES), empty_fill, jnp.float32) for _ in range(TOPM))
         best = merge_sublanes(list(lax.fori_loop(0, train_blocks, visit, none)))
-        tops[g] = jnp.concatenate([v[:1] for v in best], axis=0)
+        tops_of(g, best)
         return carry
 
     lax.fori_loop(0, groups, best_of, 0)
@@ -208,7 +224,7 @@
     def deliver(step):
         peer = lax.rem(me + step, owners)
         return pltpu.make_async_remote_copy(
-            src_ref=tops.at[peer // per_group], dst_ref=arrived.at[me],
+            src_ref=tops.at[slot(peer)], dst_ref=arrived.at[me],
             send_sem=top_send.at[peer], recv_sem=top_recv.at[me],
             device_id={"train": peer}, device_id_type=MESH,
         )
@@ -228,7 +244,7 @@
         lax.fori_loop(1, owners, body, 0)
 
     each(lambda step: deliver(step).start())
-    arrived[me] = tops[me // per_group]
+    arrived[me] = tops[slot(me)]
     for k in range(chunks):
         upward(me, k, sent)
         downward(me, k, sent)
@@ -252,16 +268,17 @@
 
     best = None
     for s in range(owners // 8):
-        lists = [arrived[s * 8:(s + 1) * 8, r, :] for r in range(TOPM)]
+        lists = []
+        for r in range(TOPM):
+            row = arrived[s * 8:(s + 1) * 8, r // per_group, :]
+            lists.append(pltpu.roll(row, (LANES - r % per_group * half) % LANES, 1))
         best = lists if best is None else merge_top(best, lists)
     best = merge_sublanes(best)
     ranked = jnp.concatenate([v[:1] for v in best], axis=0) * (1.0 / math.sqrt(K))
     square = jnp.concatenate(
         [ranked, jnp.zeros((LANES - TOPM, LANES), jnp.float32)], axis=0
     )
-    flipped[...] = square.T
-    mine = pl.multiple_of(lax.rem(me, per_group) * half, half)
-    out_ref[...] = flipped[pl.ds(mine, half), :TOPM]
+    out_ref[...] = square.T[:half, :TOPM]
     each(lambda step: deliver(step).wait_send())
 
 
@@ -280,10 +297,10 @@
     return pl.pallas_call(
         functools.partial(kernel, owners, columns, chunks),
         out_shape=jax.ShapeDtypeStruct((half, TOPM), f32),
-        in_specs=[pl.BlockSpec(memory_space=pl.ANY)] * 3
-        + [pl.BlockSpec(memory_space=pltpu.SMEM)],
+        in_specs=[pl.BlockSpec(memory_space=pl.ANY)] * 4,
         out_specs=pl.BlockSpec(memory_space=pltpu.VMEM),
         scratch_shapes=[
+            pltpu.SMEM(pairs.shape, pairs.dtype),
             pltpu.VMEM(query_grads.shape, query_grads.dtype),
             pltpu.VMEM(precond.shape, precond.dtype),
             pltpu.VMEM(train_grads.shape, train_grads.dtype),
@@ -291,10 +308,9 @@
             pltpu.VMEM((groups, rows, LANES), f32),
             pltpu.VMEM((groups, rows, LANES), f32),
             pltpu.VMEM((rows, LANES), f32),
-            pltpu.VMEM((groups, TOPM, LANES), f32),
-            pltpu.VMEM((owners, TOPM, LANES), f32),
-            pltpu.VMEM((LANES, LANES), f32),
-            pltpu.SemaphoreType.DMA((3,)),
+            pltpu.VMEM((owners, TOPM * half // LANES, LANES), f32),
+            pltpu.VMEM((owners, TOPM * half // LANES, LANES), f32),
+            pltpu.SemaphoreType.DMA((4,)),
             pltpu.SemaphoreType.DMA((1 + columns, owners, chunks)),
             pltpu.SemaphoreType.DMA((owners, chunks)),
             pltpu.SemaphoreType.DMA((groups,)),
@@ -303,7 +319,7 @@
             pltpu.SemaphoreType.DMA((owners,)),
         ],
         compiler_params=pltpu.CompilerParams(
-            collective_id=0, has_side_effects=True, vmem_limit_bytes=48 * 1024 * 1024
+            collective_id=0, has_side_effects=True, vmem_limit_bytes=63 * 1024 * 1024
         ),
     )(query_grads, precond, train_grads, pairs)
 

time: 35.4 us -> 31.2 us (0.88)
  local copies, waits for them, and re-layouts: 5.75 us -> 2.65 us
  Pallas kernels: 29.4 us -> 28.3 us
    unnamed x8 -> x2, local copies, waits for them, and re-layouts: 5.75 us -> 2.65 us
    pallas_call x1, Pallas kernels: 29.4 us -> 28.3 us  [per_device(): pl.pallas_call(functools.partial(kernel, owners, columns, chunks), out_sh...]
where the time goes in v2:
time: 31.2 us; the launch traced here: 31 us
  Pallas kernels  28.3 us (91%)
  local copies, waits for them, and re-layouts  2.65 us (8%)
    pallas_call x1, Pallas kernels, per_device(): pl.pallas_call(functools.partial(kernel, owners, columns, chunks), out_sh...  28.3 us
    unnamed x2, local copies, waits for them, and re-layouts  2.65 us

profile of v2, /device:TPU:0, one launch (start us, length us, event | category | flops | bytes accessed | tf_op | source)
XLA Modules:
  0.0 31.0 jit_solution(11623560518248286259)
XLA Ops:
  0.0 1.4 %copy.5.pairs_hbm = s32[6,2]{1,0:T(8,128)} copy(s32[6,2]{0,1:T(2,128)} %param.7) | data formatting | bytes 96 | tf_op args[3]
  1.4 28.3 %shard_map.46 = f32[16,16]{1,0:T(8,128)} custom-call(bf16[32,2048]{1,0:T(8,128)(2,1)} %query_hbm.1, bf16[4,512,512]{2,1,0:T(8,128)(2,1)} %precond_hbm.1, bf16[768,2048]{1,0:T(8,128)(2,1)} %train_hbm.1, s32[6,2]{1,0:T(8,128)} %copy.5.pairs_hbm), custom_call_target="tpu_custom_call" | custom-call | tf_op jit(solution)/shard_map/pallas_call | solution.py:297
  29.7 1.3 %copy.7 = f32[16,16]{1,0:T(8,128)} copy(f32[16,16]{1,0:T(8,128)} %shard_map.46) | data formatting | bytes 2048

commit v3 on v2

--- a/solution.py
+++ b/solution.py
@@ -102,8 +102,8 @@
         ).astype(jnp.bfloat16)
         gathered[0, me, :, j * size:(j + 1) * size] = part[:half]
         gathered[1, me, :, j * size:(j + 1) * size] = part[half:]
-    below, above = (z + levels - 1) // levels, (2 * levels - 2 - z) // levels
-    pl.semaphore_wait(barrier, columns + below + above)
+    lower, upper = (z + levels - 1) // levels, (2 * levels - 2 - z) // levels
+    pl.semaphore_wait(barrier, columns + lower + upper)
 
     def piece(owner, k, way, peer):
         ref = gathered.at[:, owner, :, pl.ds(k * chunk, chunk)]
@@ -127,43 +127,31 @@
         def _():
             act(piece(owner, k, 1, me - columns))
 
+    def below(hop, k, before, act):
+        @pl.when(z - hop >= 0)
+        def _():
+            owner = me - hop * columns
+            before(owner)
+            upward(owner, k, act)
+            across(owner, k, act)
+
+    def above(hop, k, before, act):
+        @pl.when(z + hop < levels)
+        def _():
+            owner = me + hop * columns
+            before(owner)
+            downward(owner, k, act)
+            across(owner, k, act)
+
     start = lambda copy: copy.start()
     sent = lambda copy: copy.wait_send()
     landed = lambda copy: copy.wait_recv()
 
-    for k in range(chunks):
-        upward(me, k, start)
-        downward(me, k, start)
-        across(me, k, start)
-
-    def relay(hop, carry):
-        for k in range(chunks):
-            @pl.when(z - hop >= 0)
-            def _():
-                owner = me - hop * columns
-                landed(piece(owner, k, 0, me))
-                upward(owner, k, start)
-                across(owner, k, start)
-
-            @pl.when(z + hop < levels)
-            def _():
-                owner = me + hop * columns
-                landed(piece(owner, k, 1, me))
-                downward(owner, k, start)
-                across(owner, k, start)
-        return carry
-
-    lax.fori_loop(1, levels, relay, 0)
-
-    def collect(level, carry):
+    def collect(k):
         for j in range(1, columns):
-            for k in range(chunks):
-                landed(piece(level * columns + lax.rem(x + j, columns), k, 1 + j, me))
-        return carry
-
-    lax.fori_loop(0, levels, collect, 0)
-    loads[2].wait()
-    loads[3].wait()
+            for step in range(levels):
+                owner = lax.rem(z + step, levels) * columns + lax.rem(x + j, columns)
+                landed(piece(owner, k, 1 + j, me))
 
     def trade(g):
         return pltpu.make_async_remote_copy(
@@ -172,18 +160,47 @@
             device_id={"query": 1 - core}, device_id_type=MESH,
         )
 
-    def product(which, g):
-        rows = gathered[which, pl.ds(g * per_group, per_group)].reshape(LANES, width)
+    def product(which, g, k):
+        part = slice(k * chunk, (k + 1) * chunk)
+        rows = gathered[which, pl.ds(g * per_group, per_group), :, part].reshape(LANES, chunk)
         return lax.dot_general(
-            train_v[...], rows, (((1,), (1,)), ((), ())), preferred_element_type=jnp.float32
-        )
-
-    def first(g, carry):
-        outgoing[g] = product(1 - core, g)
-        trade(g).start()
-        return carry
-
-    lax.fori_loop(0, groups, first, 0)
+            train_v[:, part], rows, (((1,), (1,)), ((), ())), preferred_element_type=jnp.float32
+        )
+
+    def multiply(k):
+        collect(k)
+        if k == 0:
+            loads[2].wait()
+
+        def other(g, carry):
+            found = product(1 - core, g, k)
+            outgoing[g] = found if k == 0 else outgoing[g] + found
+            if k == chunks - 1:
+                trade(g).start()
+            return carry
+
+        def own(g, carry):
+            found = product(core, g, k)
+            scores[g] = found if k == 0 else scores[g] + found
+            return carry
+
+        lax.fori_loop(0, groups, other, 0)
+        lax.fori_loop(0, groups, own, 0)
+
+    for wave in range(levels + chunks - 1):
+        if wave < chunks:
+            upward(me, wave, start)
+            downward(me, wave, start)
+            across(me, wave, start)
+        for hop in range(1, levels):
+            k = wave - hop
+            if 0 <= k < chunks:
+                below(hop, k, lambda owner: landed(piece(owner, k, 0, me)), start)
+                above(hop, k, lambda owner: landed(piece(owner, k, 1, me)), start)
+        if 0 <= wave - levels < chunks:
+            multiply(wave - levels)
+    multiply(chunks - 1)
+    loads[3].wait()
 
     def slot(owner):
         return owner // per_group * per_group + per_group - 1 - lax.rem(owner, per_group)
@@ -199,7 +216,6 @@
             tops[pl.ds(g * per_group, per_group), h, :] = packed
 
     def best_of(g, carry):
-        scores[...] = product(core, g)
         trade(g).wait()
         lane_owner = g * per_group + lax.broadcasted_iota(jnp.int32, (8, LANES), 1) // half
 
@@ -210,7 +226,7 @@
             vals = []
             for i in range(TBLK // 8):
                 at = pl.ds(pl.multiple_of(b * TBLK + i * 8, 8), 8)
-                total = scores[at, :] + incoming[g, at, :]
+                total = scores[g, at, :] + incoming[g, at, :]
                 vals.append(jnp.where(named, total, empty_fill))
             return tuple(merge_top(list(best), sort_falling(vals)))
 
@@ -249,21 +265,10 @@
         upward(me, k, sent)
         downward(me, k, sent)
         across(me, k, sent)
-
-    def drain(hop, carry):
-        for k in range(chunks):
-            @pl.when(z - hop >= 0)
-            def _():
-                upward(me - hop * columns, k, sent)
-                across(me - hop * columns, k, sent)
-
-            @pl.when(z + hop < levels)
-            def _():
-                downward(me + hop * columns, k, sent)
-                across(me + hop * columns, k, sent)
-        return carry
-
-    lax.fori_loop(1, levels, drain, 0)
+        for hop in range(1, levels):
+            below(hop, k, lambda owner: None, sent)
+            above(hop, k, lambda owner: None, sent)
+
     each(lambda step: receive(step).wait_recv())
 
     best = None
@@ -290,7 +295,7 @@
             columns = c
     queries, width = query_grads.shape
     rows = train_grads.shape[0]
-    chunks = 4 if owners <= 8 else 1
+    chunks = 2 if owners <= 8 else 1
     half = queries // 2
     groups = owners * half // LANES
     f32 = jnp.float32
@@ -307,7 +312,7 @@
             pltpu.VMEM((2, owners, half, width), jnp.bfloat16),
             pltpu.VMEM((groups, rows, LANES), f32),
             pltpu.VMEM((groups, rows, LANES), f32),
-            pltpu.VMEM((rows, LANES), f32),
+            pltpu.VMEM((groups, rows, LANES), f32),
             pltpu.VMEM((owners, TOPM * half // LANES, LANES), f32),
             pltpu.VMEM((owners, TOPM * half // LANES, LANES), f32),
             pltpu.SemaphoreType.DMA((4,)),

time: 31.2 us -> 29.6 us (0.949)
  Pallas kernels: 28.3 us -> 26.8 us
    pallas_call x1, Pallas kernels: 28.3 us -> 26.8 us  [per_device(): pl.pallas_call(functools.partial(kernel, owners, columns, chunks), out_sh...]
where the time goes in v3:
time: 29.6 us; the launch traced here: 29.4 us
  Pallas kernels  26.8 us (91%)
  local copies, waits for them, and re-layouts  2.65 us (9%)
    pallas_call x1, Pallas kernels, per_device(): pl.pallas_call(functools.partial(kernel, owners, columns, chunks), out_sh...  26.8 us
    unnamed x2, local copies, waits for them, and re-layouts  2.65 us

profile of v3, /device:TPU:0, one launch (start us, length us, event | category | flops | bytes accessed | tf_op | source)
XLA Modules:
  0.0 29.4 jit_solution(13165941728163405074)
XLA Ops:
  0.0 1.4 %copy.5.pairs_hbm = s32[6,2]{1,0:T(8,128)} copy(s32[6,2]{0,1:T(2,128)} %param.7) | data formatting | bytes 96 | tf_op args[3]
  1.4 26.8 %shard_map.46 = f32[16,16]{1,0:T(8,128)} custom-call(bf16[32,2048]{1,0:T(8,128)(2,1)} %query_hbm.1, bf16[4,512,512]{2,1,0:T(8,128)(2,1)} %precond_hbm.1, bf16[768,2048]{1,0:T(8,128)(2,1)} %train_hbm.1, s32[6,2]{1,0:T(8,128)} %copy.5.pairs_hbm), custom_call_target="tpu_custom_call" | custom-call | tf_op jit(solution)/shard_map/pallas_call | solution.py:302
  28.1 1.3 %copy.7 = f32[16,16]{1,0:T(8,128)} copy(f32[16,16]{1,0:T(8,128)} %shard_map.46) | data formatting | bytes 2048

commit v4 on v3

--- a/solution.py
+++ b/solution.py
@@ -187,18 +187,24 @@
         lax.fori_loop(0, groups, other, 0)
         lax.fori_loop(0, groups, own, 0)
 
-    for wave in range(levels + chunks - 1):
-        if wave < chunks:
-            upward(me, wave, start)
-            downward(me, wave, start)
-            across(me, wave, start)
+    for k in range(chunks):
+        upward(me, k, start)
+        downward(me, k, start)
+        across(me, k, start)
+    for hop in range(1, levels):
+        for k in range(chunks):
+            below(hop, k, lambda owner: landed(piece(owner, k, 0, me)), start)
+            above(hop, k, lambda owner: landed(piece(owner, k, 1, me)), start)
+    for k in range(chunks - 1):
+        multiply(k)
+    for k in range(chunks):
+        upward(me, k, sent)
+        downward(me, k, sent)
+        across(me, k, sent)
         for hop in range(1, levels):
-            k = wave - hop
-            if 0 <= k < chunks:
-                below(hop, k, lambda owner: landed(piece(owner, k, 0, me)), start)
-                above(hop, k, lambda owner: landed(piece(owner, k, 1, me)), start)
-        if 0 <= wave - levels < chunks:
-            multiply(wave - levels)
+            below(hop, k, lambda owner: None, sent)
+            above(hop, k, lambda owner: None, sent)
+
     multiply(chunks - 1)
     loads[3].wait()
 
@@ -261,14 +267,6 @@
 
     each(lambda step: deliver(step).start())
     arrived[me] = tops[slot(me)]
-    for k in range(chunks):
-        upward(me, k, sent)
-        downward(me, k, sent)
-        across(me, k, sent)
-        for hop in range(1, levels):
-            below(hop, k, lambda owner: None, sent)
-            above(hop, k, lambda owner: None, sent)
-
     each(lambda step: receive(step).wait_recv())
 
     best = None

time: 29.6 us -> 29.7 us (level)
  no operation moved by 1% of the time
where the time goes in v4:
time: 29.7 us; the launch traced here: 29.4 us
  Pallas kernels  26.8 us (90%)
  local copies, waits for them, and re-layouts  2.65 us (9%)
    pallas_call x1, Pallas kernels, per_device(): pl.pallas_call(functools.partial(kernel, owners, columns, chunks), out_sh...  26.8 us
    unnamed x2, local copies, waits for them, and re-layouts  2.65 us

profile of v4, /device:TPU:0, one launch (start us, length us, event | category | flops | bytes accessed | tf_op | source)
XLA Modules:
  0.0 29.4 jit_solution(3625371248723645298)
XLA Ops:
  0.0 1.4 %copy.5.pairs_hbm = s32[6,2]{1,0:T(8,128)} copy(s32[6,2]{0,1:T(2,128)} %param.7) | data formatting | bytes 96 | tf_op args[3]
  1.4 26.8 %shard_map.46 = f32[16,16]{1,0:T(8,128)} custom-call(bf16[32,2048]{1,0:T(8,128)(2,1)} %query_hbm.1, bf16[4,512,512]{2,1,0:T(8,128)(2,1)} %precond_hbm.1, bf16[768,2048]{1,0:T(8,128)(2,1)} %train_hbm.1, s32[6,2]{1,0:T(8,128)} %copy.5.pairs_hbm), custom_call_target="tpu_custom_call" | custom-call | tf_op jit(solution)/shard_map/pallas_call | solution.py:300
  28.1 1.3 %copy.7 = f32[16,16]{1,0:T(8,128)} copy(f32[16,16]{1,0:T(8,128)} %shard_map.46) | data formatting | bytes 2048
